TPU v7x, 32 devices: a whole 2x2x4 slice. The times are simulated.
32 devices in a mesh: grp: 16 (over z, y, x), fold: 2 (over core).
Axes of the slice: x: 2, y: 2, z: 4, core: 2. Of those that a mesh axis runs over, the one named last changes fastest.
Arguments:
- blocks: bfloat16 [9, 2, 64, 64, 2048], P(None, None, 'fold', None, 'grp'), may hold values from -30 to 30
- source: bfloat16 [2, 64, 12, 2048], P(None, 'fold', None, 'grp'), may hold values from -8 to 8
- plane_counts: int32 [16], P('grp'), may hold values from 1 to 2, 24 in all
Outputs:
- solution: float32 [2, 64, 12, 2048], P(None, 'fold', None, 'grp')
- residual: float32 [2, 64, 12, 2048], P(None, 'fold', None, 'grp')
Inputs may be any that keep to these rules, and one draw needn't show every extreme that they name: plane_counts sum to 24; the busiest group holds exactly 2 planes.
All inputs are finite; a program needn't handle non-finite values.
Results may differ from a plain program's by a relative error of at most 0.0032.
Values may be sent and summed in bfloat16 or wider, within the bound.
A program may use at most 128 MiB of HBM per device.

v0:
```python
import functools

import jax
import jax.numpy as jnp
import numpy as np
from jax import lax
from jax.experimental import pallas as pl
from jax.experimental.pallas import tpu as pltpu
from jax.sharding import PartitionSpec as P

SWEEPS = 2
CHUNK = 8
GROUPS = 16
HALF = GROUPS // 2
LOCAL = (0, 1, 2, 3, 4, 7, 8)
ACROSS = (5, 6)
MESH = pl.DeviceIdType.MESH


def lane_moves():
    moves = np.zeros((256, 512), np.float32)
    for lane in range(128):
        base, site = lane // 8 * 8, lane % 8
        low = site < 4
        moves[base + (site ^ 4) + (0 if low else 128), lane] = 1
        moves[base + (site ^ 4) + (128 if low else 0), 128 + lane] = 1
        moves[base + (site & 4) + ((site + 1) & 3), 256 + lane] = 1
        moves[base + (site & 4) + ((site - 1) & 3), 384 + lane] = 1
    return jnp.asarray(moves, jnp.bfloat16)


def kernel(n_grp, n_fold, counts, blocks, source, moves, sol, res,
           raw, w_local, w_across, image, gath, last, rims, local_rhs, red,
           load_sem, x_send, x_recv, r_send, r_recv, s_send, s_recv):
    bf16, f32 = jnp.bfloat16, jnp.float32
    rows, comps = blocks.shape[2], blocks.shape[3]
    nrhs = source.shape[1]
    total = n_grp * n_fold
    grp, fold = lax.axis_index("grp"), lax.axis_index("fold")
    me = grp * n_fold + fold
    loads = [pltpu.make_async_copy(blocks.at[m], raw.at[m], load_sem.at[m]) for m in range(9)]
    for load in loads:
        load.start()

    def device(index):
        return (lax.div(index, n_fold), lax.rem(index, n_fold))

    barrier = pltpu.get_barrier_semaphore()

    def greet(d, carry):
        pl.semaphore_signal(barrier, inc=1, device_id=device(lax.rem(me + d, total)), device_id_type=MESH)
        return carry

    lax.fori_loop(1, total, greet, 0)

    live = (counts[0] - 1).astype(f32)
    lane = lax.broadcasted_iota(jnp.int32, (rows, 128), 1)

    for p in range(2):
        planes = [source[p, k].astype(f32) for k in range(nrhs)]
        for g in range(GROUPS):
            value = jnp.zeros((rows, 128), f32)
            for k in range(nrhs):
                shift = 8 * (k - g) % 128
                moved = planes[k] if shift == 0 else pltpu.roll(planes[k], shift, 1)
                value = jnp.where(lane // 8 == k, moved, value)
            if g >= HALF:
                value = value * live
            res[g, :, 128 * p:128 * p + 128] = value

    pl.semaphore_wait(barrier, total - 1)

    def send_parts(sweep):
        def fill(h, carry):
            lower, upper = res[h], res[h + HALF]
            gath[sweep, fold, h] = lower.astype(bf16)
            gath[sweep, fold, h + HALF] = upper.astype(bf16)
            last[sweep, h] = (upper * live + lower * (1.0 - live)).astype(bf16)
            return carry

        lax.fori_loop(0, HALF, fill, 0, unroll=2)
        gathers, edges = [], []
        for d in range(1, n_fold):
            gathers.append(pltpu.make_async_remote_copy(
                src_ref=gath.at[sweep, fold], dst_ref=gath.at[sweep, fold],
                send_sem=x_send.at[sweep, d], recv_sem=x_recv.at[sweep, d],
                device_id=(grp, lax.rem(fold + d, n_fold)), device_id_type=MESH))
        for side, src, step in ((0, gath.at[sweep, fold, pl.ds(0, HALF)], n_grp - 1), (1, last.at[sweep], 1)):
            edges.append(pltpu.make_async_remote_copy(
                src_ref=src, dst_ref=rims.at[sweep, side, fold],
                send_sem=r_send.at[sweep, side, 0], recv_sem=r_recv.at[sweep, side, 0],
                device_id=(lax.rem(grp + step, n_grp), fold), device_id_type=MESH))
        for copy in edges + gathers:
            copy.start()
        return gathers, edges

    def wait_gather(sweep):
        for d in range(1, n_fold):
            sender = lax.rem(fold + n_fold - d, n_fold)
            slot = gath.at[sweep, sender]
            pltpu.make_async_remote_copy(
                src_ref=slot, dst_ref=slot, send_sem=x_send.at[sweep, d], recv_sem=x_recv.at[sweep, d],
                device_id=(grp, lax.rem(fold + d, n_fold)), device_id_type=MESH).wait_recv()

    def forward(sweep, side, d, sender):
        slot = rims.at[sweep, side, sender]
        return pltpu.make_async_remote_copy(
            src_ref=slot, dst_ref=slot, send_sem=r_send.at[sweep, side, d],
            recv_sem=r_recv.at[sweep, side, d],
            device_id=(grp, lax.rem(fold + d, n_fold)), device_id_type=MESH)

    def pass_edges(sweep, edges):
        passed = []
        for side in range(2):
            edges[side].wait_recv()
            passed += [forward(sweep, side, d, fold) for d in range(1, n_fold)]
            for copy in passed[-(n_fold - 1):]:
                copy.start()
        return passed

    def wait_edges(sweep):
        for side in range(2):
            for d in range(1, n_fold):
                forward(sweep, side, d, lax.rem(fold + n_fold - d, n_fold)).wait_recv()

    def whole_rows(read):
        parts = [read(f) for f in range(n_fold)]
        if rows % 16:
            return jnp.concatenate([part.astype(f32) for part in parts], axis=0).astype(bf16)
        return jnp.concatenate(parts, axis=0)

    def doubled(re, im):
        return jnp.concatenate(
            [jnp.concatenate([re, im], axis=1), jnp.concatenate([-im, re], axis=1)], axis=0)

    def build_local(sweep):
        def pair(h, carry):
            chunks = [whole_rows(lambda f, i=i: gath[sweep, f, 2 * h + i]) for i in range(2)]
            (are, aim), (bre, bim) = [(c[:, :128], c[:, 128:]) for c in chunks]
            local_rhs[0, 2 * h] = doubled(are, aim)
            local_rhs[0, 2 * h + 1] = doubled(bre, bim)
            left = jnp.concatenate([jnp.concatenate([are, aim, bre, bim], axis=0),
                                    jnp.concatenate([bre, bim, are, aim], axis=0)], axis=1)
            moved = jnp.dot(left, moves[...], preferred_element_type=f32).astype(bf16)
            for i in range(2):
                for hop in range(4):
                    cut = moved[2 * comps * i:2 * comps * (i + 1), 128 * hop:128 * hop + 128]
                    local_rhs[1 + hop, 2 * h + i] = doubled(cut[:comps], cut[comps:])
            return carry

        lax.fori_loop(0, HALF, pair, 0, unroll=2)

    row_site = lax.broadcasted_iota(jnp.int32, (rows * CHUNK, 256), 0) % CHUNK
    lane_site = lax.broadcasted_iota(jnp.int32, (rows * CHUNK, 256), 1) % CHUNK

    def same_site(product):
        kept = jnp.where(row_site == lane_site, product, 0.0)
        return jnp.sum(kept.reshape(rows, CHUNK, 256), axis=1)

    def apply_local(begin, end):
        def chunk(g, carry):
            plane, x, low = g // HALF * HALF, g % HALF // 2, g % 2
            ahead, behind = plane + (x + 1) % 4 * 2 + low, plane + (x + 3) % 4 * 2 + low
            rhs = jnp.concatenate(
                [local_rhs[0, g], local_rhs[0, ahead], local_rhs[0, behind]]
                + [local_rhs[1 + hop, g] for hop in range(4)], axis=0)
            image[g] = same_site(jnp.dot(w_local[g], rhs, preferred_element_type=f32))
            return carry

        lax.fori_loop(begin, end, chunk, 0, unroll=8)

    def dots(a, r):
        are, aim, rre, rim = a[:, :128], a[:, 128:], r[:, :128], r[:, 128:]
        return are * rre + aim * rim, are * rim - aim * rre, are * are + aim * aim

    def apply_across(sweep):
        def plane_chunk(h, sums):
            after = whole_rows(lambda f: rims[sweep, 0, f, h])
            before = whole_rows(lambda f: rims[sweep, 1, f, h])
            after = doubled(after[:, :128], after[:, 128:])
            before = doubled(before[:, :128], before[:, 128:])
            inner, outer = local_rhs[0, h], local_rhs[0, h + HALF]
            up = (outer.astype(f32) * live + after.astype(f32) * (1.0 - live)).astype(bf16)
            first = same_site(jnp.dot(w_across[h], jnp.concatenate([up, before], axis=0),
                                      preferred_element_type=f32))
            second = same_site(jnp.dot(w_across[h + HALF], jnp.concatenate([after, inner], axis=0),
                                       preferred_element_type=f32))
            first = first + image[h]
            second = (second + image[h + HALF]) * live
            image[h] = first
            image[h + HALF] = second
            one, two = dots(first, res[h]), dots(second, res[h + HALF])
            return tuple(s + a + b for s, a, b in zip(sums, one, two))

        zero = jnp.zeros((rows, 128), f32)
        return lax.fori_loop(0, HALF, plane_chunk, (zero, zero, zero), unroll=4)

    row8 = lax.broadcasted_iota(jnp.int32, (8, 128), 0)
    lane8 = lax.broadcasted_iota(jnp.int32, (8, 128), 1)

    def reduce_all(sweep, sums):
        re, im, norm = [jnp.sum(s, axis=0, keepdims=True) for s in sums]
        red[sweep, 0] = jnp.where(row8 == 0, re, jnp.where(row8 == 1, im, norm))

        def send(d, carry):
            pltpu.make_async_remote_copy(
                src_ref=red.at[sweep, 0], dst_ref=red.at[sweep, d],
                send_sem=s_send.at[sweep], recv_sem=s_recv.at[sweep],
                device_id=device(lax.rem(me + d, total)), device_id_type=MESH).start()
            return carry

        lax.fori_loop(1, total, send, 0)
        everyone = red.at[sweep, pl.ds(1, total - 1)]
        pltpu.make_async_copy(everyone, everyone, s_recv.at[sweep]).wait()
        value = jnp.sum(red[sweep], axis=0)
        for step in (4, 2, 1):
            value = value + jnp.where(lane8 // step % 2 == 0,
                                      pltpu.roll(value, 128 - step, 1), pltpu.roll(value, step, 1))
        real = lane8[:1] < 8 * nrhs
        norm = jnp.where(real, value[2:3], 1.0)
        pltpu.make_async_copy(everyone, everyone, s_send.at[sweep]).wait()
        return value[0:1] / norm, value[1:2] / norm

    def turned(alpha_re, alpha_im, v):
        re, im = v[:, :128], v[:, 128:]
        return jnp.concatenate([alpha_re * re - alpha_im * im, alpha_re * im + alpha_im * re], axis=1)

    for sweep in range(SWEEPS):
        gathers, edges = send_parts(sweep)
        if sweep == 0:
            for m in range(9):
                loads[m].wait()
                place = LOCAL.index(m) if m in LOCAL else ACROSS.index(m)
                target = w_local if m in LOCAL else w_across

                def two_rows(i, carry, m=m, place=place, target=target):
                    flipped = []
                    for a in range(2):
                        both = jnp.concatenate([raw[m, 0, 2 * i + a], raw[m, 1, 2 * i + a]], axis=0)
                        flipped.append(both.T.astype(f32))
                    for g in range(GROUPS):
                        piece = jnp.concatenate([f[8 * g:8 * g + 8] for f in flipped], axis=0)
                        target[g, pl.ds(pl.multiple_of(16 * i, 16), 16),
                               2 * comps * place:2 * comps * (place + 1)] = piece.astype(bf16)
                    return carry

                lax.fori_loop(0, rows // 2, two_rows, 0, unroll=4)
            passed = pass_edges(sweep, edges)
        wait_gather(sweep)
        build_local(sweep)
        apply_local(0, HALF)
        if sweep > 0:
            passed = pass_edges(sweep, edges)
        apply_local(HALF, GROUPS)
        wait_edges(sweep)
        sums = apply_across(sweep)
        alpha_re, alpha_im = reduce_all(sweep, sums)

        def update(g, carry):
            r = res[g]
            step = turned(alpha_re, alpha_im, r)
            sol[g] = step if sweep == 0 else sol[g] + step
            res[g] = r - turned(alpha_re, alpha_im, image[g])
            return carry

        lax.fori_loop(0, GROUPS, update, 0, unroll=4)
        for copy in gathers + edges + passed:
            copy.wait_send()


def finish(sol, res, sol_out, res_out):
    nrhs = sol_out.shape[1]
    lane = lax.broadcasted_iota(jnp.int32, (sol.shape[1], 128), 1)
    for held, out in ((sol, sol_out), (res, res_out)):
        for p in range(2):
            chunks = [held[g, :, 128 * p:128 * p + 128] for g in range(GROUPS)]
            for k in range(nrhs):
                value = chunks[0] if k == 0 else pltpu.roll(chunks[0], -8 * k % 128, 1)
                for g in range(1, GROUPS):
                    shift = 8 * (g - k) % 128
                    moved = chunks[g] if shift == 0 else pltpu.roll(chunks[g], shift, 1)
                    value = jnp.where(lane // 8 == g, moved, value)
                out[p, k] = value


def body(n_grp, n_fold, blocks, source, plane_counts):
    rows, comps = blocks.shape[2], blocks.shape[3]
    nrhs = source.shape[2]
    bf16, f32 = jnp.bfloat16, jnp.float32
    shape = (2, nrhs, rows, GROUPS * CHUNK)
    vmem = pl.BlockSpec(memory_space=pltpu.VMEM)
    total = n_grp * n_fold
    held = jax.ShapeDtypeStruct((GROUPS, rows, 256), f32)
    iterate = pl.pallas_call(
        functools.partial(kernel, n_grp, n_fold),
        out_shape=(held, held),
        in_specs=[pl.BlockSpec(memory_space=pltpu.SMEM), pl.BlockSpec(memory_space=pl.ANY), vmem, vmem],
        out_specs=(vmem, vmem),
        scratch_shapes=[
            pltpu.VMEM(blocks.shape, bf16),
            pltpu.VMEM((GROUPS, rows * CHUNK, len(LOCAL) * 2 * comps), bf16),
            pltpu.VMEM((GROUPS, rows * CHUNK, len(ACROSS) * 2 * comps), bf16),
            pltpu.VMEM((GROUPS, rows, 256), f32),
            pltpu.VMEM((SWEEPS, n_fold, GROUPS, rows, 256), bf16),
            pltpu.VMEM((SWEEPS, HALF, rows, 256), bf16),
            pltpu.VMEM((SWEEPS, 2, n_fold, HALF, rows, 256), bf16),
            pltpu.VMEM((5, GROUPS, 2 * comps, 256), bf16),
            pltpu.VMEM((SWEEPS, total, 8, 128), f32),
            pltpu.SemaphoreType.DMA((9,)),
            pltpu.SemaphoreType.DMA((SWEEPS, n_fold)),
            pltpu.SemaphoreType.DMA((SWEEPS, n_fold)),
            pltpu.SemaphoreType.DMA((SWEEPS, 2, n_fold)),
            pltpu.SemaphoreType.DMA((SWEEPS, 2, n_fold)),
            pltpu.SemaphoreType.DMA((SWEEPS,)),
            pltpu.SemaphoreType.DMA((SWEEPS,)),
        ],
        compiler_params=pltpu.CompilerParams(
            collective_id=0, has_side_effects=True, vmem_limit_bytes=56 * 1024 * 1024),
    )(plane_counts, blocks, source.transpose(0, 2, 1, 3), lane_moves())
    outs = pl.pallas_call(
        finish,
        out_shape=(jax.ShapeDtypeStruct(shape, f32), jax.ShapeDtypeStruct(shape, f32)),
        in_specs=[vmem, vmem],
        out_specs=(vmem, vmem),
    )(*iterate)
    return tuple(out.transpose(0, 2, 1, 3) for out in outs)


def solution(mesh):
    return jax.shard_map(
        functools.partial(body, mesh.shape["grp"], mesh.shape["fold"]),
        mesh=mesh,
        in_specs=(P(None, None, "fold", None, "grp"), P(None, "fold", None, "grp"), P("grp")),
        out_specs=(P(None, "fold", None, "grp"), P(None, "fold", None, "grp")),
        check_vma=False,
    )
```

profile of v0, /device:TPU:0, one launch (start us, length us, event | category | flops | bytes accessed | tf_op | source)
XLA Modules:
  0.0 50.6 jit_solution(17148842970554666862)
XLA Ops:
  1.3 44.2 %shard_map.59 = (f32[16,32,256]{2,1,0:T(8,128)}, f32[16,32,256]{2,1,0:T(8,128)}) custom-call(s32[1]{0:T(128)S(6)} %copy.6.counts, bf16[9,2,32,64,128]{4,3,2,1,0:T(8,128)(2,1)} %blocks.1, bf16[2,12,32,128]{3,2,1,0:T(8,128)(2,1)} %bitcast.3, bf16[256,512]{1,0:T(8,128)(2,1)} %constant.2.clone.moves), custom_call_target="tpu_custom_call" | custom-call | tf_op jit(solution)/shard_map/pallas_call | solution.py:294
  45.5 5.1 %shard_map.60 = (f32[2,12,32,128]{3,2,1,0:T(8,128)}, f32[2,12,32,128]{3,2,1,0:T(8,128)}) custom-call(f32[16,32,256]{2,1,0:T(8,128)} %get-tuple-element.6.sol, f32[16,32,256]{2,1,0:T(8,128)} %get-tuple-element.7.res), custom_call_target="tpu_custom_call" | custom-call | tf_op jit(solution)/shard_map/pallas_call | solution.py:320
where the time goes:
time: 50.7 us; the launch traced here: 50.6 us
  Pallas kernels  49.3 us (97%)
  between operations  1.28 us (3%)
    pallas_call x1, Pallas kernels, body(): pl.pallas_call(functools.partial(kernel, n_grp, n_fold), out_shape=(held,...  44.2 us
    pallas_call x1, Pallas kernels, body(): pl.pallas_call(finish, out_shape=(jax.ShapeDtypeStruct(shape, f32), jax.S...  5.07 us

commit v1 on v0

v1 whole, which is shorter than its diff:
```python
import functools

import jax
import jax.numpy as jnp
import numpy as np
from jax import lax
from jax.experimental import pallas as pl
from jax.experimental.pallas import tpu as pltpu
from jax.sharding import PartitionSpec as P

SWEEPS = 2
CHUNK = 8
GROUPS = 16
HALF = GROUPS // 2
LOCAL = (0, 1, 2, 3, 4, 7, 8)
ACROSS = (5, 6)
MESH = pl.DeviceIdType.MESH


def lane_moves():
    moves = np.zeros((256, 512), np.float32)
    for lane in range(128):
        base, site = lane // 8 * 8, lane % 8
        low = site < 4
        moves[base + (site ^ 4) + (0 if low else 128), lane] = 1
        moves[base + (site ^ 4) + (128 if low else 0), 128 + lane] = 1
        moves[base + (site & 4) + ((site + 1) & 3), 256 + lane] = 1
        moves[base + (site & 4) + ((site - 1) & 3), 384 + lane] = 1
    return jnp.asarray(moves, jnp.bfloat16)


def swap_blocks(tiles):
    tiles = list(tiles)
    block = lax.broadcasted_iota(jnp.int32, tiles[0].shape, 1) // CHUNK
    for bit in (1, 2, 4, 8):
        high = block // bit % 2 == 1
        for i in range(GROUPS):
            if i & bit == 0:
                a, b = tiles[i], tiles[i | bit]
                tiles[i] = jnp.where(high, pltpu.roll(b, CHUNK * bit, 1), a)
                tiles[i | bit] = jnp.where(high, b, pltpu.roll(a, 128 - CHUNK * bit, 1))
    return tiles


def turned(alpha_re, alpha_im, v):
    re, im = v[:, :128], v[:, 128:]
    return jnp.concatenate([alpha_re * re - alpha_im * im, alpha_re * im + alpha_im * re], axis=1)


def kernel(n_grp, n_fold, counts, blocks, source, moves, res_out, image_out, alphas,
           raw, w_local, w_across, image, res, first_image, gath, last, edge_image, rims, local_rhs, red,
           load_sem, x_send, x_recv, r_send, r_recv, s_send, s_recv):
    bf16, f32 = jnp.bfloat16, jnp.float32
    rows, comps = blocks.shape[2], blocks.shape[3]
    nrhs = source.shape[1]
    total = n_grp * n_fold
    grp, fold = lax.axis_index("grp"), lax.axis_index("fold")
    me = grp * n_fold + fold
    loads = [pltpu.make_async_copy(blocks.at[m], raw.at[m], load_sem.at[m]) for m in range(9)]
    for load in loads:
        load.start()

    def device(index):
        return (lax.div(index, n_fold), lax.rem(index, n_fold))

    barrier = pltpu.get_barrier_semaphore()

    def greet(d, carry):
        pl.semaphore_signal(barrier, inc=1, device_id=device(lax.rem(me + d, total)), device_id_type=MESH)
        return carry

    lax.fori_loop(1, total, greet, 0, unroll=total <= 64)

    live = (counts[0] - 1).astype(f32)

    for p in range(2):
        planes = [source[p, k].astype(f32) for k in range(nrhs)]
        for t in range(0, rows, 8):
            tiles = [plane[t:t + 8] for plane in planes]
            tiles += [jnp.zeros((8, 128), f32)] * (GROUPS - nrhs)
            for g, tile in enumerate(swap_blocks(tiles)):
                res[g, t:t + 8, 128 * p:128 * p + 128] = tile * live if g >= HALF else tile

    pl.semaphore_wait(barrier, total - 1)

    def exchange(sweep, mine, slots, first_plane, last_plane):
        copies = []
        for side, src, step in ((0, first_plane, n_grp - 1), (1, last_plane, 1)):
            copies.append(pltpu.make_async_remote_copy(
                src_ref=src, dst_ref=rims.at[sweep, side, fold],
                send_sem=r_send.at[sweep, side, 0], recv_sem=r_recv.at[sweep, side, 0],
                device_id=(lax.rem(grp + step, n_grp), fold), device_id_type=MESH))
        for d in range(1, n_fold):
            copies.append(pltpu.make_async_remote_copy(
                src_ref=mine, dst_ref=slots.at[fold],
                send_sem=x_send.at[sweep, d], recv_sem=x_recv.at[sweep, d],
                device_id=(grp, lax.rem(fold + d, n_fold)), device_id_type=MESH))
        for copy in copies:
            copy.start()
        return copies

    def send_source():
        def fill(h, carry):
            lower, upper = res[h], res[h + HALF]
            gath[fold, h] = lower.astype(bf16)
            gath[fold, h + HALF] = upper.astype(bf16)
            last[h] = (upper * live + lower * (1.0 - live)).astype(bf16)
            return carry

        lax.fori_loop(0, HALF, fill, 0, unroll=2)
        return exchange(0, gath.at[fold], gath, gath.at[fold, pl.ds(0, HALF)], last)

    def send_image():
        return exchange(1, first_image.at[fold], first_image, edge_image.at[0], edge_image.at[1])

    def wait_gather(sweep, slots):
        for d in range(1, n_fold):
            slot = slots.at[lax.rem(fold + n_fold - d, n_fold)]
            pltpu.make_async_remote_copy(
                src_ref=slot, dst_ref=slot, send_sem=x_send.at[sweep, d], recv_sem=x_recv.at[sweep, d],
                device_id=(grp, lax.rem(fold + d, n_fold)), device_id_type=MESH).wait_recv()

    def forward(sweep, side, d, sender):
        slot = rims.at[sweep, side, sender]
        return pltpu.make_async_remote_copy(
            src_ref=slot, dst_ref=slot, send_sem=r_send.at[sweep, side, d],
            recv_sem=r_recv.at[sweep, side, d],
            device_id=(grp, lax.rem(fold + d, n_fold)), device_id_type=MESH)

    def pass_edges(sweep, edges):
        passed = []
        for side in range(2):
            edges[side].wait_recv()
            passed += [forward(sweep, side, d, fold) for d in range(1, n_fold)]
            for copy in passed[-(n_fold - 1):]:
                copy.start()
        return passed

    def wait_edges(sweep):
        for side in range(2):
            for d in range(1, n_fold):
                forward(sweep, side, d, lax.rem(fold + n_fold - d, n_fold)).wait_recv()

    def whole_rows(read):
        parts = [read(f) for f in range(n_fold)]
        if rows % 16:
            return jnp.concatenate([part.astype(f32) for part in parts], axis=0).astype(bf16)
        return jnp.concatenate(parts, axis=0)

    def doubled(re, im):
        return jnp.concatenate(
            [jnp.concatenate([re, im], axis=1), jnp.concatenate([-im, re], axis=1)], axis=0)

    def stepped(alpha, start, moved):
        parts = [start(f).astype(f32) - turned(*alpha, moved(f).astype(f32)) for f in range(n_fold)]
        return jnp.concatenate(parts, axis=0).astype(bf16)

    def build_local(alpha):
        def pair(h, carry):
            if alpha is None:
                chunks = [whole_rows(lambda f, i=i: gath[f, 2 * h + i]) for i in range(2)]
            else:
                chunks = []
                for g in (2 * h, 2 * h + 1):
                    res[g] = res[g] - turned(*alpha, first_image[fold, g])
                    chunks.append(stepped(alpha, lambda f, g=g: gath[f, g], lambda f, g=g: first_image[f, g]))
            (are, aim), (bre, bim) = [(c[:, :128], c[:, 128:]) for c in chunks]
            local_rhs[0, 2 * h] = doubled(are, aim)
            local_rhs[0, 2 * h + 1] = doubled(bre, bim)
            left = jnp.concatenate([jnp.concatenate([are, aim, bre, bim], axis=0),
                                    jnp.concatenate([bre, bim, are, aim], axis=0)], axis=1)
            moved = jnp.dot(left, moves[...], preferred_element_type=f32).astype(bf16)
            for i in range(2):
                for hop in range(4):
                    cut = moved[2 * comps * i:2 * comps * (i + 1), 128 * hop:128 * hop + 128]
                    local_rhs[1 + hop, 2 * h + i] = doubled(cut[:comps], cut[comps:])
            return carry

        lax.fori_loop(0, HALF, pair, 0, unroll=2)

    row_site = lax.broadcasted_iota(jnp.int32, (rows * CHUNK, 256), 0) % CHUNK
    lane_site = lax.broadcasted_iota(jnp.int32, (rows * CHUNK, 256), 1) % CHUNK

    def same_site(product):
        kept = jnp.where(row_site == lane_site, product, 0.0)
        return jnp.sum(kept.reshape(rows, CHUNK, 256), axis=1)

    def apply_local(begin, end):
        def chunk(g, carry):
            plane, x, low = g // HALF * HALF, g % HALF // 2, g % 2
            ahead, behind = plane + (x + 1) % 4 * 2 + low, plane + (x + 3) % 4 * 2 + low
            rhs = jnp.concatenate(
                [local_rhs[0, g], local_rhs[0, ahead], local_rhs[0, behind]]
                + [local_rhs[1 + hop, g] for hop in range(4)], axis=0)
            image[g] = same_site(jnp.dot(w_local[g], rhs, preferred_element_type=f32))
            return carry

        lax.fori_loop(begin, end, chunk, 0, unroll=8)

    def dots(a, r):
        are, aim, rre, rim = a[:, :128], a[:, 128:], r[:, :128], r[:, 128:]
        return are * rre + aim * rim, are * rim - aim * rre, are * are + aim * aim

    def apply_across(alpha):
        def plane_chunk(h, sums):
            if alpha is None:
                after, before = [whole_rows(lambda f, side=side: rims[0, side, f, h]) for side in range(2)]
            else:
                after, before = [stepped(alpha, lambda f, side=side: rims[0, side, f, h],
                                         lambda f, side=side: rims[1, side, f, h]) for side in range(2)]
            after = doubled(after[:, :128], after[:, 128:])
            before = doubled(before[:, :128], before[:, 128:])
            inner, outer = local_rhs[0, h], local_rhs[0, h + HALF]
            up = (outer.astype(f32) * live + after.astype(f32) * (1.0 - live)).astype(bf16)
            first = same_site(jnp.dot(w_across[h], jnp.concatenate([up, before], axis=0),
                                      preferred_element_type=f32))
            second = same_site(jnp.dot(w_across[h + HALF], jnp.concatenate([after, inner], axis=0),
                                       preferred_element_type=f32))
            first = first + image[h]
            second = (second + image[h + HALF]) * live
            if alpha is None:
                first_image[fold, h] = first
                first_image[fold, h + HALF] = second
                edge_image[0, h] = first.astype(bf16)
                edge_image[1, h] = (second + first * (1.0 - live)).astype(bf16)
            else:
                image[h] = first
                image[h + HALF] = second
            one, two = dots(first, res[h]), dots(second, res[h + HALF])
            return tuple(s + a + b for s, a, b in zip(sums, one, two))

        zero = jnp.zeros((rows, 128), f32)
        return lax.fori_loop(0, HALF, plane_chunk, (zero, zero, zero), unroll=4)

    row8 = lax.broadcasted_iota(jnp.int32, (8, 128), 0)
    lane8 = lax.broadcasted_iota(jnp.int32, (8, 128), 1)

    def spread(value):
        for step in (4, 2, 1):
            value = value + jnp.where(lane8 // step % 2 == 0,
                                      pltpu.roll(value, 128 - step, 1), pltpu.roll(value, step, 1))
        return value

    def send_sums(sweep, sums):
        re, im, norm = [jnp.sum(s, axis=0, keepdims=True) for s in sums]
        value = spread(jnp.where(row8 == 0, re, jnp.where(row8 == 1, im, norm)))
        spot = lane8[:1] % CHUNK
        red[sweep, 0] = jnp.where(spot == 0, value[0:1], jnp.where(spot == 1, value[1:2], value[2:3]))

        def send(d, carry):
            pltpu.make_async_remote_copy(
                src_ref=red.at[sweep, 0], dst_ref=red.at[sweep, d],
                send_sem=s_send.at[sweep], recv_sem=s_recv.at[sweep],
                device_id=device(lax.rem(me + d, total)), device_id_type=MESH).start()
            return carry

        lax.fori_loop(1, total, send, 0, unroll=total <= 64)

    def wait_sums(sweep):
        everyone = red.at[sweep, pl.ds(1, total - 1)]
        pltpu.make_async_copy(everyone, everyone, s_recv.at[sweep]).wait()
        value = jnp.broadcast_to(jnp.sum(red[sweep], axis=0), (8, 128))
        value = spread(jnp.where(lane8 % CHUNK == row8, value, 0.0))
        norm = jnp.where(lane8[:1] < CHUNK * nrhs, value[2:3], 1.0)
        return value[0:1] / norm, value[1:2] / norm

    def natural(held, out):
        for p in range(2):
            for t in range(0, rows, 8):
                tiles = swap_blocks([held[g, t:t + 8, 128 * p:128 * p + 128] for g in range(GROUPS)])
                for k in range(nrhs):
                    out[p, k, t:t + 8] = tiles[k]

    copies = send_source()
    for m in range(9):
        loads[m].wait()
        place = LOCAL.index(m) if m in LOCAL else ACROSS.index(m)
        target = w_local if m in LOCAL else w_across

        def two_rows(i, carry, m=m, place=place, target=target):
            flipped = []
            for a in range(2):
                both = jnp.concatenate([raw[m, 0, 2 * i + a], raw[m, 1, 2 * i + a]], axis=0)
                flipped.append(both.T.astype(f32))
            for g in range(GROUPS):
                piece = jnp.concatenate([f[8 * g:8 * g + 8] for f in flipped], axis=0)
                target[g, pl.ds(pl.multiple_of(16 * i, 16), 16),
                       2 * comps * place:2 * comps * (place + 1)] = piece.astype(bf16)
            return carry

        lax.fori_loop(0, rows // 2, two_rows, 0, unroll=min(rows // 2, 8))
    copies += pass_edges(0, copies[:2])
    wait_gather(0, gath)
    build_local(None)
    apply_local(0, GROUPS)
    wait_edges(0)
    send_sums(0, apply_across(None))
    later = send_image()
    first = wait_sums(0)
    wait_gather(1, first_image)
    build_local(first)
    apply_local(0, HALF)
    later += pass_edges(1, later[:2])
    apply_local(HALF, GROUPS)
    wait_edges(1)
    send_sums(1, apply_across(first))
    natural(res, res_out)
    natural(image, image_out)
    second = wait_sums(1)
    alphas[...] = jnp.where(row8 == 0, first[0], jnp.where(row8 == 1, first[1], jnp.where(
        row8 == 2, second[0], second[1])))
    for copy in copies + later:
        copy.wait_send()
    for sweep in range(SWEEPS):
        everyone = red.at[sweep, pl.ds(1, total - 1)]
        pltpu.make_async_copy(everyone, everyone, s_send.at[sweep]).wait()


def finish(counts, source, res, image, alphas, sol_out, res_out):
    nrhs, rows = source.shape[1:3]
    f32 = jnp.float32
    live = (counts[0] - 1).astype(f32)
    lane = lax.broadcasted_iota(jnp.int32, (rows, 128), 1)
    kept = jnp.where(lane < 64, 1.0, live)
    for k in range(nrhs):
        are, aim, bre, bim = [jnp.broadcast_to(alphas[i:i + 1, CHUNK * k:CHUNK * k + 1], (rows, 128))
                              for i in range(4)]
        sre, sim = [source[p, k].astype(f32) * kept for p in range(2)]
        rre, rim, ire, iim = res[0, k], res[1, k], image[0, k], image[1, k]
        sol_out[0, k] = (are * sre - aim * sim) + (bre * rre - bim * rim)
        sol_out[1, k] = (are * sim + aim * sre) + (bre * rim + bim * rre)
        res_out[0, k] = rre - (bre * ire - bim * iim)
        res_out[1, k] = rim - (bre * iim + bim * ire)


def body(n_grp, n_fold, blocks, source, plane_counts):
    rows, comps = blocks.shape[2], blocks.shape[3]
    nrhs = source.shape[2]
    bf16, f32 = jnp.bfloat16, jnp.float32
    shape = (2, nrhs, rows, GROUPS * CHUNK)
    vmem = pl.BlockSpec(memory_space=pltpu.VMEM)
    total = n_grp * n_fold
    held = jax.ShapeDtypeStruct(shape, f32)
    smem = pl.BlockSpec(memory_space=pltpu.SMEM)
    source = source.transpose(0, 2, 1, 3)
    iterate = pl.pallas_call(
        functools.partial(kernel, n_grp, n_fold),
        out_shape=(held, held, jax.ShapeDtypeStruct((8, 128), f32)),
        in_specs=[smem, pl.BlockSpec(memory_space=pl.ANY), vmem, vmem],
        out_specs=(vmem, vmem, vmem),
        scratch_shapes=[
            pltpu.VMEM(blocks.shape, bf16),
            pltpu.VMEM((GROUPS, rows * CHUNK, len(LOCAL) * 2 * comps), bf16),
            pltpu.VMEM((GROUPS, rows * CHUNK, len(ACROSS) * 2 * comps), bf16),
            pltpu.VMEM((GROUPS, rows, 256), f32),
            pltpu.VMEM((GROUPS, rows, 256), f32),
            pltpu.VMEM((n_fold, GROUPS, rows, 256), f32),
            pltpu.VMEM((n_fold, GROUPS, rows, 256), bf16),
            pltpu.VMEM((HALF, rows, 256), bf16),
            pltpu.VMEM((2, HALF, rows, 256), bf16),
            pltpu.VMEM((SWEEPS, 2, n_fold, HALF, rows, 256), bf16),
            pltpu.VMEM((5, GROUPS, 2 * comps, 256), bf16),
            pltpu.VMEM((SWEEPS, total, 1, 128), f32),
            pltpu.SemaphoreType.DMA((9,)),
            pltpu.SemaphoreType.DMA((SWEEPS, n_fold)),
            pltpu.SemaphoreType.DMA((SWEEPS, n_fold)),
            pltpu.SemaphoreType.DMA((SWEEPS, 2, n_fold)),
            pltpu.SemaphoreType.DMA((SWEEPS, 2, n_fold)),
            pltpu.SemaphoreType.DMA((SWEEPS,)),
            pltpu.SemaphoreType.DMA((SWEEPS,)),
        ],
        compiler_params=pltpu.CompilerParams(
            collective_id=0, has_side_effects=True, vmem_limit_bytes=56 * 1024 * 1024),
    )(plane_counts, blocks, source, lane_moves())
    outs = pl.pallas_call(
        finish,
        out_shape=(jax.ShapeDtypeStruct(shape, f32), jax.ShapeDtypeStruct(shape, f32)),
        in_specs=[smem, vmem, vmem, vmem, vmem],
        out_specs=(vmem, vmem),
        compiler_params=pltpu.CompilerParams(vmem_limit_bytes=8 * 1024 * 1024),
    )(plane_counts, source, *iterate)
    return tuple(out.transpose(0, 2, 1, 3) for out in outs)


def solution(mesh):
    return jax.shard_map(
        functools.partial(body, mesh.shape["grp"], mesh.shape["fold"]),
        mesh=mesh,
        in_specs=(P(None, None, "fold", None, "grp"), P(None, "fold", None, "grp"), P("grp")),
        out_specs=(P(None, "fold", None, "grp"), P(None, "fold", None, "grp")),
        check_vma=False,
    )
```

time: 50.7 us -> 43.3 us (0.85)
  Pallas kernels: 49.3 us -> 39 us
  local copies, waits for them, and re-layouts: 0 us -> 2.67 us
    pallas_call x1, Pallas kernels: 44.2 us -> 37.9 us  [body(): pl.pallas_call(functools.partial(kernel, n_grp, n_fold), out_shape=(held,...]
    pallas_call x1, Pallas kernels: 5.07 us -> 1.13 us  [body(): pl.pallas_call(finish, out_shape=(jax.ShapeDtypeStruct(shape, f32), jax.S...]
    unnamed x0 -> x8, local copies, waits for them, and re-layouts: none -> 2.67 us
where the time goes in v1:
time: 43.3 us; the launch traced here: 43 us
  Pallas kernels  39 us (90%)
  local copies, waits for them, and re-layouts  2.67 us (6%)
  between operations  1.35 us (3%)
    pallas_call x1, Pallas kernels, body(): pl.pallas_call(functools.partial(kernel, n_grp, n_fold), out_shape=(held,...  37.9 us
    unnamed x8, local copies, waits for them, and re-layouts  2.67 us
    pallas_call x1, Pallas kernels, body(): pl.pallas_call(finish, out_shape=(jax.ShapeDtypeStruct(shape, f32), jax.S...  1.13 us

profile of v1, /device:TPU:0, one launch (start us, length us, event | category | flops | bytes accessed | tf_op | source)
XLA Modules:
  0.0 43.0 jit_solution(5309599701867389365)
XLA Ops:
  0.6 0.0 copy-start
  1.3 37.9 %shard_map.59 = (f32[2,12,32,128]{3,2,1,0:T(8,128)}, f32[2,12,32,128]{3,2,1,0:T(8,128)}, f32[8,128]{1,0:T(8,128)}) custom-call(s32[1]{0:T(128)S(6)} %copy.6.counts, bf16[9,2,32,64,128]{4,3,2,1,0:T(8,128)(2,1)} %blocks.1, bf16[2,12,32,128]{3,2,1,0:T(8,128)(2,1)} %bitcast.3, bf16[256,512]{1,0:T(8,128)(2,1)} %constant.2.clone.moves), custom_call_target="tpu_custom_call" | custom-call | tf_op jit(solution)/shard_map/pallas_call | solution.py:346
  39.2 0.0 copy-done
  39.2 0.0 copy-start.1
  39.2 1.0 %copy-done.1 = f32[2,12,32,128]{3,2,1,0:T(8,128)S(1)} copy-done((f32[2,12,32,128]{3,2,1,0:T(8,128)S(1)}, f32[2,12,32,128]{3,2,1,0:T(8,128)}, u32[]{:S(2)}) %copy-start.1) | copy-done | bytes 393240
  40.2 0.0 copy-start.2
  40.2 1.0 %copy-done.2 = f32[2,12,32,128]{3,2,1,0:T(8,128)S(1)} copy-done((f32[2,12,32,128]{3,2,1,0:T(8,128)S(1)}, f32[2,12,32,128]{3,2,1,0:T(8,128)}, u32[]{:S(2)}) %copy-start.2) | copy-done | bytes 393240
  41.2 0.0 copy-start.3
  41.2 0.7 %copy-done.3 = f32[8,128]{1,0:T(8,128)S(1)} copy-done((f32[8,128]{1,0:T(8,128)S(1)}, f32[8,128]{1,0:T(8,128)}, u32[]{:S(2)}) %copy-start.3) | copy-done | bytes 4120
  41.9 1.1 %shard_map.60 = (f32[2,12,32,128]{3,2,1,0:T(8,128)}, f32[2,12,32,128]{3,2,1,0:T(8,128)}) custom-call(s32[1]{0:T(128)S(6)} %copy.6.counts, bf16[2,12,32,128]{3,2,1,0:T(8,128)(2,1)S(1)} %bitcast.4, f32[2,12,32,128]{3,2,1,0:T(8,128)S(1)} %copy-done.1, f32[2,12,32,128]{3,2,1,0:T(8,128)S(1)} %copy-done.2, f32[8,128]{1,0:T(8,128)S(1)} %copy-done.3), custom_call_target="tpu_custom_call" | custom-call | tf_op jit(solution)/shard_map/pallas_call | solution.py:375
Async XLA Ops:
  0.6 38.6 %copy-start = (bf16[2,32,12,128]{3,1,2,0:T(8,128)(2,1)S(1)}, bf16[2,32,12,128]{3,1,2,0:T(8,128)(2,1)}, u32[]{:S(2)}) copy-start(bf16[2,32,12,128]{3,1,2,0:T(8,128)(2,1)} %param.5) | copy-start | bytes 589828
  39.2 1.0 %copy-start.1 = (f32[2,12,32,128]{3,2,1,0:T(8,128)S(1)}, f32[2,12,32,128]{3,2,1,0:T(8,128)}, u32[]{:S(2)}) copy-start(f32[2,12,32,128]{3,2,1,0:T(8,128)} %get-tuple-element.7.res) | copy-start | bytes 1179652
  40.2 1.0 %copy-start.2 = (f32[2,12,32,128]{3,2,1,0:T(8,128)S(1)}, f32[2,12,32,128]{3,2,1,0:T(8,128)}, u32[]{:S(2)}) copy-start(f32[2,12,32,128]{3,2,1,0:T(8,128)} %get-tuple-element.8.image) | copy-start | bytes 1179652
  41.2 0.7 %copy-start.3 = (f32[8,128]{1,0:T(8,128)S(1)}, f32[8,128]{1,0:T(8,128)}, u32[]{:S(2)}) copy-start(f32[8,128]{1,0:T(8,128)} %get-tuple-element.9.alphas) | copy-start | bytes 12292

commit v2 on v1

--- a/solution.py
+++ b/solution.py
@@ -17,16 +17,15 @@
 MESH = pl.DeviceIdType.MESH
 
 
-def lane_moves():
-    moves = np.zeros((256, 512), np.float32)
-    for lane in range(128):
-        base, site = lane // 8 * 8, lane % 8
-        low = site < 4
-        moves[base + (site ^ 4) + (0 if low else 128), lane] = 1
-        moves[base + (site ^ 4) + (128 if low else 0), 128 + lane] = 1
-        moves[base + (site & 4) + ((site + 1) & 3), 256 + lane] = 1
-        moves[base + (site & 4) + ((site - 1) & 3), 384 + lane] = 1
-    return jnp.asarray(moves, jnp.bfloat16)
+def lane_moves(hop):
+    row = lax.broadcasted_iota(jnp.int32, (256, 128), 0)
+    lane = lax.broadcasted_iota(jnp.int32, (256, 128), 1)
+    base, site = lane // 8 * 8, lane % 8
+    low, plane = site // 4 == 0, site // 4 * 4
+    across = base + (site + 4) % 8
+    origin = (jnp.where(low, across, across + 128), jnp.where(low, across + 128, across),
+              base + plane + (site + 1) % 4, base + plane + (site + 3) % 4)[hop]
+    return jnp.where(row == origin, 1.0, 0.0).astype(jnp.bfloat16)
 
 
 def swap_blocks(tiles):
@@ -47,8 +46,8 @@
     return jnp.concatenate([alpha_re * re - alpha_im * im, alpha_re * im + alpha_im * re], axis=1)
 
 
-def kernel(n_grp, n_fold, counts, blocks, source, moves, res_out, image_out, alphas,
-           raw, w_local, w_across, image, res, first_image, gath, last, edge_image, rims, local_rhs, red,
+def kernel(n_grp, n_fold, counts, blocks, source, res_out, image_out, alphas,
+           moves, raw, w_local, w_across, image, res, first_image, gath, last, edge_image, rims, local_rhs, red,
            load_sem, x_send, x_recv, r_send, r_recv, s_send, s_recv):
     bf16, f32 = jnp.bfloat16, jnp.float32
     rows, comps = blocks.shape[2], blocks.shape[3]
@@ -272,6 +271,8 @@
                     out[p, k, t:t + 8] = tiles[k]
 
     copies = send_source()
+    for hop in range(4):
+        moves[:, 128 * hop:128 * hop + 128] = lane_moves(hop)
     for m in range(9):
         loads[m].wait()
         place = LOCAL.index(m) if m in LOCAL else ACROSS.index(m)
@@ -308,7 +309,7 @@
     natural(image, image_out)
     second = wait_sums(1)
     alphas[...] = jnp.where(row8 == 0, first[0], jnp.where(row8 == 1, first[1], jnp.where(
-        row8 == 2, second[0], second[1])))
+        row8 == 2, second[0], jnp.where(row8 == 3, second[1], jnp.where(lane8 < 64, 1.0, live)))))
     for copy in copies + later:
         copy.wait_send()
     for sweep in range(SWEEPS):
@@ -316,12 +317,10 @@
         pltpu.make_async_copy(everyone, everyone, s_send.at[sweep]).wait()
 
 
-def finish(counts, source, res, image, alphas, sol_out, res_out):
+def finish(source, res, image, alphas, sol_out, res_out):
     nrhs, rows = source.shape[1:3]
     f32 = jnp.float32
-    live = (counts[0] - 1).astype(f32)
-    lane = lax.broadcasted_iota(jnp.int32, (rows, 128), 1)
-    kept = jnp.where(lane < 64, 1.0, live)
+    kept = jnp.broadcast_to(alphas[4:5], (rows, 128))
     for k in range(nrhs):
         are, aim, bre, bim = [jnp.broadcast_to(alphas[i:i + 1, CHUNK * k:CHUNK * k + 1], (rows, 128))
                               for i in range(4)]
@@ -346,9 +345,10 @@
     iterate = pl.pallas_call(
         functools.partial(kernel, n_grp, n_fold),
         out_shape=(held, held, jax.ShapeDtypeStruct((8, 128), f32)),
-        in_specs=[smem, pl.BlockSpec(memory_space=pl.ANY), vmem, vmem],
+        in_specs=[smem, pl.BlockSpec(memory_space=pl.ANY), vmem],
         out_specs=(vmem, vmem, vmem),
         scratch_shapes=[
+            pltpu.VMEM((256, 512), bf16),
             pltpu.VMEM(blocks.shape, bf16),
             pltpu.VMEM((GROUPS, rows * CHUNK, len(LOCAL) * 2 * comps), bf16),
             pltpu.VMEM((GROUPS, rows * CHUNK, len(ACROSS) * 2 * comps), bf16),
@@ -370,15 +370,15 @@
             pltpu.SemaphoreType.DMA((SWEEPS,)),
         ],
         compiler_params=pltpu.CompilerParams(
-            collective_id=0, has_side_effects=True, vmem_limit_bytes=56 * 1024 * 1024),
-    )(plane_counts, blocks, source, lane_moves())
+            collective_id=0, has_side_effects=True, vmem_limit_bytes=52 * 1024 * 1024),
+    )(plane_counts, blocks, source)
     outs = pl.pallas_call(
         finish,
         out_shape=(jax.ShapeDtypeStruct(shape, f32), jax.ShapeDtypeStruct(shape, f32)),
-        in_specs=[smem, vmem, vmem, vmem, vmem],
+        in_specs=[vmem] * 4,
         out_specs=(vmem, vmem),
         compiler_params=pltpu.CompilerParams(vmem_limit_bytes=8 * 1024 * 1024),
-    )(plane_counts, source, *iterate)
+    )(source, *iterate)
     return tuple(out.transpose(0, 2, 1, 3) for out in outs)
 
 

time: 43.3 us -> 39.4 us (0.910)
  Pallas kernels: 39 us -> 37.1 us
  local copies, waits for them, and re-layouts: 2.67 us -> 0.92 us
    pallas_call x1, Pallas kernels: 37.9 us -> 35.9 us  [body(): pl.pallas_call(functools.partial(kernel, n_grp, n_fold), out_shape=(held,...]
    unnamed x8 -> x2, local copies, waits for them, and re-layouts: 2.67 us -> 0.92 us
where the time goes in v2:
time: 39.4 us; the launch traced here: 39.3 us
  Pallas kernels  37.1 us (94%)
  between operations  1.29 us (3%)
  local copies, waits for them, and re-layouts  0.92 us (2%)
    pallas_call x1, Pallas kernels, body(): pl.pallas_call(functools.partial(kernel, n_grp, n_fold), out_shape=(held,...  35.9 us
    pallas_call x1, Pallas kernels, body(): pl.pallas_call(finish, out_shape=(jax.ShapeDtypeStruct(shape, f32), jax.S...  1.13 us
    unnamed x2, local copies, waits for them, and re-layouts  0.92 us

profile of v2, /device:TPU:0, one launch (start us, length us, event | category | flops | bytes accessed | tf_op | source)
XLA Modules:
  0.0 39.3 jit_solution(8989517960265509876)
XLA Ops:
  1.3 0.0 copy-start
  1.3 0.9 %copy-done = bf16[2,32,12,128]{3,1,2,0:T(8,128)(2,1)S(1)} copy-done((bf16[2,32,12,128]{3,1,2,0:T(8,128)(2,1)S(1)}, bf16[2,32,12,128]{3,1,2,0:T(8,128)(2,1)}, u32[]{:S(2)}) %copy-start) | copy-done | bytes 196632
  2.2 35.9 %shard_map.50 = (f32[2,12,32,128]{3,2,1,0:T(8,128)S(1)}, f32[2,12,32,128]{3,2,1,0:T(8,128)S(1)}, f32[8,128]{1,0:T(8,128)S(1)}) custom-call(s32[1]{0:T(128)S(6)} %copy.5.counts, bf16[9,2,32,64,128]{4,3,2,1,0:T(8,128)(2,1)} %blocks.1, bf16[2,12,32,128]{3,2,1,0:T(8,128)(2,1)S(1)} %bitcast.3), custom_call_target="tpu_custom_call" | custom-call | tf_op jit(solution)/shard_map/pallas_call | solution.py:345
  38.1 1.1 %shard_map.51 = (f32[2,12,32,128]{3,2,1,0:T(8,128)}, f32[2,12,32,128]{3,2,1,0:T(8,128)}) custom-call(bf16[2,12,32,128]{3,2,1,0:T(8,128)(2,1)S(1)} %bitcast.4, f32[2,12,32,128]{3,2,1,0:T(8,128)S(1)} %get-tuple-element.7.res, f32[2,12,32,128]{3,2,1,0:T(8,128)S(1)} %get-tuple-element.8.image, f32[8,128]{1,0:T(8,128)S(1)} %get-tuple-element.9.alphas), custom_call_target="tpu_custom_call" | custom-call | tf_op jit(solution)/shard_map/pallas_call | solution.py:375
Async XLA Ops:
  1.3 0.9 %copy-start = (bf16[2,32,12,128]{3,1,2,0:T(8,128)(2,1)S(1)}, bf16[2,32,12,128]{3,1,2,0:T(8,128)(2,1)}, u32[]{:S(2)}) copy-start(bf16[2,32,12,128]{3,1,2,0:T(8,128)(2,1)} %param.4) | copy-start | bytes 589828

commit v3 on v2

--- a/solution.py
+++ b/solution.py
@@ -56,9 +56,6 @@
     grp, fold = lax.axis_index("grp"), lax.axis_index("fold")
     me = grp * n_fold + fold
     loads = [pltpu.make_async_copy(blocks.at[m], raw.at[m], load_sem.at[m]) for m in range(9)]
-    for load in loads:
-        load.start()
-
     def device(index):
         return (lax.div(index, n_fold), lax.rem(index, n_fold))
 
@@ -69,6 +66,8 @@
         return carry
 
     lax.fori_loop(1, total, greet, 0, unroll=total <= 64)
+    for load in loads:
+        load.start()
 
     live = (counts[0] - 1).astype(f32)
 
@@ -126,13 +125,20 @@
             recv_sem=r_recv.at[sweep, side, d],
             device_id=(grp, lax.rem(fold + d, n_fold)), device_id_type=MESH)
 
-    def pass_edges(sweep, edges):
-        passed = []
-        for side in range(2):
-            edges[side].wait_recv()
-            passed += [forward(sweep, side, d, fold) for d in range(1, n_fold)]
-            for copy in passed[-(n_fold - 1):]:
-                copy.start()
+    def pass_edge(sweep, side, edges):
+        edges[side].wait_recv()
+        passed = [forward(sweep, side, d, fold) for d in range(1, n_fold)]
+        for copy in passed:
+            copy.start()
+        return passed
+
+    def local_and_pass(sweep, edges):
+        apply_local(0, 8)
+        passed = pass_edge(sweep, 0, edges)
+        apply_local(8, 12)
+        passed += pass_edge(sweep, 1, edges)
+        apply_local(12, 16)
+        wait_edges(sweep)
         return passed
 
     def wait_edges(sweep):
@@ -177,12 +183,26 @@
 
         lax.fori_loop(0, HALF, pair, 0, unroll=2)
 
-    row_site = lax.broadcasted_iota(jnp.int32, (rows * CHUNK, 256), 0) % CHUNK
-    lane_site = lax.broadcasted_iota(jnp.int32, (rows * CHUNK, 256), 1) % CHUNK
+    row_site = lax.broadcasted_iota(jnp.int32, (8, 256), 0)
+    lane_site = lax.broadcasted_iota(jnp.int32, (8, 256), 1) % CHUNK
+    upper = {bit: row_site // bit % 2 == 1 for bit in (4, 2, 1)}
+    stays = {bit: row_site // bit % 2 == lane_site // bit % 2 for bit in (4, 2, 1)}
 
     def same_site(product):
-        kept = jnp.where(row_site == lane_site, product, 0.0)
-        return jnp.sum(kept.reshape(rows, CHUNK, 256), axis=1)
+        out = []
+        for t in range(0, rows, 8):
+            parts = [product[CHUNK * (t + r):CHUNK * (t + r + 1)] for r in range(8)]
+            for bit in (4, 2, 1):
+                merged = []
+                for a, b in zip(parts[:bit], parts[bit:]):
+                    here = jnp.where(upper[bit], b, a)
+                    there = pltpu.roll(jnp.where(upper[bit], a, b), 4 if bit == 4 else bit, 0)
+                    if bit != 4:
+                        there = jnp.where(upper[bit], there, pltpu.roll(jnp.where(upper[bit], a, b), 8 - bit, 0))
+                    merged.append(jnp.where(stays[bit], here, there))
+                parts = merged
+            out.append(parts[0])
+        return out[0] if len(out) == 1 else jnp.concatenate(out, axis=0)
 
     def apply_local(begin, end):
         def chunk(g, carry):
@@ -194,7 +214,7 @@
             image[g] = same_site(jnp.dot(w_local[g], rhs, preferred_element_type=f32))
             return carry
 
-        lax.fori_loop(begin, end, chunk, 0, unroll=8)
+        lax.fori_loop(begin, end, chunk, 0, unroll=end - begin)
 
     def dots(a, r):
         are, aim, rre, rim = a[:, :128], a[:, 128:], r[:, :128], r[:, 128:]
@@ -290,20 +310,15 @@
             return carry
 
         lax.fori_loop(0, rows // 2, two_rows, 0, unroll=min(rows // 2, 8))
-    copies += pass_edges(0, copies[:2])
     wait_gather(0, gath)
     build_local(None)
-    apply_local(0, GROUPS)
-    wait_edges(0)
+    copies += local_and_pass(0, copies[:2])
     send_sums(0, apply_across(None))
     later = send_image()
     first = wait_sums(0)
     wait_gather(1, first_image)
     build_local(first)
-    apply_local(0, HALF)
-    later += pass_edges(1, later[:2])
-    apply_local(HALF, GROUPS)
-    wait_edges(1)
+    later += local_and_pass(1, later[:2])
     send_sums(1, apply_across(first))
     natural(res, res_out)
     natural(image, image_out)

time: 39.4 us -> 35.3 us (0.90)
  Pallas kernels: 37.1 us -> 32.9 us
    pallas_call x1, Pallas kernels: 35.9 us -> 31.8 us  [body(): pl.pallas_call(functools.partial(kernel, n_grp, n_fold), out_shape=(held,...]
where the time goes in v3:
time: 35.3 us; the launch traced here: 35.1 us
  Pallas kernels  32.9 us (93%)
  between operations  1.29 us (4%)
  local copies, waits for them, and re-layouts  0.92 us (3%)
    pallas_call x1, Pallas kernels, body(): pl.pallas_call(functools.partial(kernel, n_grp, n_fold), out_shape=(held,...  31.8 us
    pallas_call x1, Pallas kernels, body(): pl.pallas_call(finish, out_shape=(jax.ShapeDtypeStruct(shape, f32), jax.S...  1.13 us
    unnamed x2, local copies, waits for them, and re-layouts  0.92 us

profile of v3, /device:TPU:0, one launch (start us, length us, event | category | flops | bytes accessed | tf_op | source)
XLA Modules:
  0.0 35.1 jit_solution(3290096561324949713)
XLA Ops:
  1.3 0.0 copy-start
  1.3 0.9 %copy-done = bf16[2,32,12,128]{3,1,2,0:T(8,128)(2,1)S(1)} copy-done((bf16[2,32,12,128]{3,1,2,0:T(8,128)(2,1)S(1)}, bf16[2,32,12,128]{3,1,2,0:T(8,128)(2,1)}, u32[]{:S(2)}) %copy-start) | copy-done | bytes 196632
  2.2 31.8 %shard_map.50 = (f32[2,12,32,128]{3,2,1,0:T(8,128)S(1)}, f32[2,12,32,128]{3,2,1,0:T(8,128)S(1)}, f32[8,128]{1,0:T(8,128)S(1)}) custom-call(s32[1]{0:T(128)S(6)} %copy.5.counts, bf16[9,2,32,64,128]{4,3,2,1,0:T(8,128)(2,1)} %blocks.1, bf16[2,12,32,128]{3,2,1,0:T(8,128)(2,1)S(1)} %bitcast.3), custom_call_target="tpu_custom_call" | custom-call | tf_op jit(solution)/shard_map/pallas_call | solution.py:360
  34.0 1.1 %shard_map.51 = (f32[2,12,32,128]{3,2,1,0:T(8,128)}, f32[2,12,32,128]{3,2,1,0:T(8,128)}) custom-call(bf16[2,12,32,128]{3,2,1,0:T(8,128)(2,1)S(1)} %bitcast.4, f32[2,12,32,128]{3,2,1,0:T(8,128)S(1)} %get-tuple-element.7.res, f32[2,12,32,128]{3,2,1,0:T(8,128)S(1)} %get-tuple-element.8.image, f32[8,128]{1,0:T(8,128)S(1)} %get-tuple-element.9.alphas), custom_call_target="tpu_custom_call" | custom-call | tf_op jit(solution)/shard_map/pallas_call | solution.py:390
Async XLA Ops:
  1.3 0.9 %copy-start = (bf16[2,32,12,128]{3,1,2,0:T(8,128)(2,1)S(1)}, bf16[2,32,12,128]{3,1,2,0:T(8,128)(2,1)}, u32[]{:S(2)}) copy-start(bf16[2,32,12,128]{3,1,2,0:T(8,128)(2,1)} %param.4) | copy-start | bytes 589828

commit v4 on v3

--- a/solution.py
+++ b/solution.py
@@ -41,13 +41,28 @@
     return tiles
 
 
+def pack(chunks):
+    halves = [chunk[:, 128 * p:128 * p + 128] for chunk in chunks for p in range(2)]
+    lane = lax.broadcasted_iota(jnp.int32, halves[0].shape, 1)
+    return [jnp.where(lane < 96, halves[j], pltpu.roll(halves[6 + j // 3], 96 - 32 * (j % 3), 1)) for j in range(6)]
+
+
+def unpack(tiles):
+    lane = lax.broadcasted_iota(jnp.int32, tiles[0].shape, 1)
+    halves = [jnp.where(lane < 96, tile, 0.0) for tile in tiles]
+    for a, b, c in (tiles[:3], tiles[3:]):
+        halves.append(jnp.where(lane < 32, pltpu.roll(a, 32, 1), jnp.where(
+            lane < 64, pltpu.roll(b, 64, 1), jnp.where(lane < 96, pltpu.roll(c, 96, 1), 0.0))))
+    return [jnp.concatenate(halves[2 * i:2 * i + 2], axis=1) for i in range(4)]
+
+
 def turned(alpha_re, alpha_im, v):
     re, im = v[:, :128], v[:, 128:]
     return jnp.concatenate([alpha_re * re - alpha_im * im, alpha_re * im + alpha_im * re], axis=1)
 
 
 def kernel(n_grp, n_fold, counts, blocks, source, res_out, image_out, alphas,
-           moves, raw, w_local, w_across, image, res, first_image, gath, last, edge_image, rims, local_rhs, red,
+           moves, raw, w_local, w_across, image, res, first_image, gath, edge_pack, rims, local_rhs, red,
            load_sem, x_send, x_recv, r_send, r_recv, s_send, s_recv):
     bf16, f32 = jnp.bfloat16, jnp.float32
     rows, comps = blocks.shape[2], blocks.shape[3]
@@ -81,35 +96,47 @@
 
     pl.semaphore_wait(barrier, total - 1)
 
-    def exchange(sweep, mine, slots, first_plane, last_plane):
-        copies = []
-        for side, src, step in ((0, first_plane, n_grp - 1), (1, last_plane, 1)):
-            copies.append(pltpu.make_async_remote_copy(
-                src_ref=src, dst_ref=rims.at[sweep, side, fold],
-                send_sem=r_send.at[sweep, side, 0], recv_sem=r_recv.at[sweep, side, 0],
-                device_id=(lax.rem(grp + step, n_grp), fold), device_id_type=MESH))
-        for d in range(1, n_fold):
-            copies.append(pltpu.make_async_remote_copy(
-                src_ref=mine, dst_ref=slots.at[fold],
-                send_sem=x_send.at[sweep, d], recv_sem=x_recv.at[sweep, d],
-                device_id=(grp, lax.rem(fold + d, n_fold)), device_id_type=MESH))
+    def send_edges(sweep, held):
+        def group(q, carry):
+            lower = [held(4 * q + i) for i in range(4)]
+            upper = [held(4 * q + i + HALF) for i in range(4)]
+            final = [b + a * (1.0 - live) for a, b in zip(lower, upper)]
+            for side, chunks in enumerate((lower, final)):
+                for j, tile in enumerate(pack(chunks)):
+                    edge_pack[sweep, side, q, j] = tile.astype(bf16)
+            return carry
+
+        lax.fori_loop(0, 2, group, 0, unroll=2)
+        copies = [pltpu.make_async_remote_copy(
+            src_ref=edge_pack.at[sweep, side], dst_ref=rims.at[sweep, side, fold],
+            send_sem=r_send.at[sweep, side, 0], recv_sem=r_recv.at[sweep, side, 0],
+            device_id=(lax.rem(grp + step, n_grp), fold), device_id_type=MESH)
+            for side, step in ((0, n_grp - 1), (1, 1))]
         for copy in copies:
             copy.start()
         return copies
 
+    def send_gather(sweep, slots):
+        copies = [pltpu.make_async_remote_copy(
+            src_ref=slots.at[fold], dst_ref=slots.at[fold],
+            send_sem=x_send.at[sweep, d], recv_sem=x_recv.at[sweep, d],
+            device_id=(grp, lax.rem(fold + d, n_fold)), device_id_type=MESH) for d in range(1, n_fold)]
+        for copy in copies:
+            copy.start()
+        return copies
+
     def send_source():
+        edges = send_edges(0, lambda g: res[g])
+
         def fill(h, carry):
-            lower, upper = res[h], res[h + HALF]
-            gath[fold, h] = lower.astype(bf16)
-            gath[fold, h + HALF] = upper.astype(bf16)
-            last[h] = (upper * live + lower * (1.0 - live)).astype(bf16)
-            return carry
-
-        lax.fori_loop(0, HALF, fill, 0, unroll=2)
-        return exchange(0, gath.at[fold], gath, gath.at[fold, pl.ds(0, HALF)], last)
+            gath[fold, h] = res[h].astype(bf16)
+            return carry
+
+        lax.fori_loop(0, GROUPS, fill, 0, unroll=4)
+        return edges + send_gather(0, gath)
 
     def send_image():
-        return exchange(1, first_image.at[fold], first_image, edge_image.at[0], edge_image.at[1])
+        return send_edges(1, lambda g: first_image[fold, g]) + send_gather(1, first_image)
 
     def wait_gather(sweep, slots):
         for d in range(1, n_fold):
@@ -133,11 +160,11 @@
         return passed
 
     def local_and_pass(sweep, edges):
-        apply_local(0, 8)
+        apply_local(0, 6)
         passed = pass_edge(sweep, 0, edges)
-        apply_local(8, 12)
+        apply_local(6, 10)
         passed += pass_edge(sweep, 1, edges)
-        apply_local(12, 16)
+        apply_local(10, 16)
         wait_edges(sweep)
         return passed
 
@@ -159,6 +186,14 @@
     def stepped(alpha, start, moved):
         parts = [start(f).astype(f32) - turned(*alpha, moved(f).astype(f32)) for f in range(n_fold)]
         return jnp.concatenate(parts, axis=0).astype(bf16)
+
+    def edge_chunks(alpha, side, q):
+        folds = []
+        for f in range(n_fold):
+            start, moved = [unpack([rims[sweep, side, f, q, j].astype(f32) for j in range(6)])
+                            if sweep == 0 or alpha is not None else None for sweep in range(2)]
+            folds.append(start if alpha is None else [a - turned(*alpha, b) for a, b in zip(start, moved)])
+        return [jnp.concatenate(parts, axis=0).astype(bf16) for parts in zip(*folds)]
 
     def build_local(alpha):
         def pair(h, carry):
@@ -221,12 +256,7 @@
         return are * rre + aim * rim, are * rim - aim * rre, are * are + aim * aim
 
     def apply_across(alpha):
-        def plane_chunk(h, sums):
-            if alpha is None:
-                after, before = [whole_rows(lambda f, side=side: rims[0, side, f, h]) for side in range(2)]
-            else:
-                after, before = [stepped(alpha, lambda f, side=side: rims[0, side, f, h],
-                                         lambda f, side=side: rims[1, side, f, h]) for side in range(2)]
+        def plane_chunk(h, after, before, sums):
             after = doubled(after[:, :128], after[:, 128:])
             before = doubled(before[:, :128], before[:, 128:])
             inner, outer = local_rhs[0, h], local_rhs[0, h + HALF]
@@ -240,8 +270,6 @@
             if alpha is None:
                 first_image[fold, h] = first
                 first_image[fold, h + HALF] = second
-                edge_image[0, h] = first.astype(bf16)
-                edge_image[1, h] = (second + first * (1.0 - live)).astype(bf16)
             else:
                 image[h] = first
                 image[h + HALF] = second
@@ -249,7 +277,14 @@
             return tuple(s + a + b for s, a, b in zip(sums, one, two))
 
         zero = jnp.zeros((rows, 128), f32)
-        return lax.fori_loop(0, HALF, plane_chunk, (zero, zero, zero), unroll=4)
+
+        def group(q, sums):
+            sides = [edge_chunks(alpha, side, q) for side in range(2)]
+            for i in range(4):
+                sums = plane_chunk(4 * q + i, sides[0][i], sides[1][i], sums)
+            return sums
+
+        return lax.fori_loop(0, 2, group, (zero, zero, zero))
 
     row8 = lax.broadcasted_iota(jnp.int32, (8, 128), 0)
     lane8 = lax.broadcasted_iota(jnp.int32, (8, 128), 1)
@@ -371,9 +406,8 @@
             pltpu.VMEM((GROUPS, rows, 256), f32),
             pltpu.VMEM((n_fold, GROUPS, rows, 256), f32),
             pltpu.VMEM((n_fold, GROUPS, rows, 256), bf16),
-            pltpu.VMEM((HALF, rows, 256), bf16),
-            pltpu.VMEM((2, HALF, rows, 256), bf16),
-            pltpu.VMEM((SWEEPS, 2, n_fold, HALF, rows, 256), bf16),
+            pltpu.VMEM((SWEEPS, 2, 2, 6, rows, 128), bf16),
+            pltpu.VMEM((SWEEPS, 2, n_fold, 2, 6, rows, 128), bf16),
             pltpu.VMEM((5, GROUPS, 2 * comps, 256), bf16),
             pltpu.VMEM((SWEEPS, total, 1, 128), f32),
             pltpu.SemaphoreType.DMA((9,)),

time: 35.3 us -> 34.8 us (0.986)
  Pallas kernels: 32.9 us -> 32.4 us
    pallas_call x1, Pallas kernels: 31.8 us -> 31.3 us  [body(): pl.pallas_call(functools.partial(kernel, n_grp, n_fold), out_shape=(held,...]
where the time goes in v4:
time: 34.8 us; the launch traced here: 34.6 us
  Pallas kernels  32.4 us (93%)
  between operations  1.29 us (4%)
  local copies, waits for them, and re-layouts  0.92 us (3%)
    pallas_call x1, Pallas kernels, body(): pl.pallas_call(functools.partial(kernel, n_grp, n_fold), out_shape=(held,...  31.3 us
    pallas_call x1, Pallas kernels, body(): pl.pallas_call(finish, out_shape=(jax.ShapeDtypeStruct(shape, f32), jax.S...  1.13 us
    unnamed x2, local copies, waits for them, and re-layouts  0.92 us

profile of v4, /device:TPU:0, one launch (start us, length us, event | category | flops | bytes accessed | tf_op | source)
XLA Modules:
  0.0 34.6 jit_solution(11201896731731508537)
XLA Ops:
  1.3 0.0 copy-start
  1.3 0.9 %copy-done = bf16[2,32,12,128]{3,1,2,0:T(8,128)(2,1)S(1)} copy-done((bf16[2,32,12,128]{3,1,2,0:T(8,128)(2,1)S(1)}, bf16[2,32,12,128]{3,1,2,0:T(8,128)(2,1)}, u32[]{:S(2)}) %copy-start) | copy-done | bytes 196632
  2.2 31.3 %shard_map.50 = (f32[2,12,32,128]{3,2,1,0:T(8,128)S(1)}, f32[2,12,32,128]{3,2,1,0:T(8,128)S(1)}, f32[8,128]{1,0:T(8,128)S(1)}) custom-call(s32[1]{0:T(128)S(6)} %copy.5.counts, bf16[9,2,32,64,128]{4,3,2,1,0:T(8,128)(2,1)} %blocks.1, bf16[2,12,32,128]{3,2,1,0:T(8,128)(2,1)S(1)} %bitcast.3), custom_call_target="tpu_custom_call" | custom-call | tf_op jit(solution)/shard_map/pallas_call | solution.py:395
  33.5 1.1 %shard_map.51 = (f32[2,12,32,128]{3,2,1,0:T(8,128)}, f32[2,12,32,128]{3,2,1,0:T(8,128)}) custom-call(bf16[2,12,32,128]{3,2,1,0:T(8,128)(2,1)S(1)} %bitcast.4, f32[2,12,32,128]{3,2,1,0:T(8,128)S(1)} %get-tuple-element.7.res, f32[2,12,32,128]{3,2,1,0:T(8,128)S(1)} %get-tuple-element.8.image, f32[8,128]{1,0:T(8,128)S(1)} %get-tuple-element.9.alphas), custom_call_target="tpu_custom_call" | custom-call | tf_op jit(solution)/shard_map/pallas_call | solution.py:424
Async XLA Ops:
  1.3 0.9 %copy-start = (bf16[2,32,12,128]{3,1,2,0:T(8,128)(2,1)S(1)}, bf16[2,32,12,128]{3,1,2,0:T(8,128)(2,1)}, u32[]{:S(2)}) copy-start(bf16[2,32,12,128]{3,1,2,0:T(8,128)(2,1)} %param.4) | copy-start | bytes 589828

commit v5 on v4

--- a/solution.py
+++ b/solution.py
@@ -61,15 +61,17 @@
     return jnp.concatenate([alpha_re * re - alpha_im * im, alpha_re * im + alpha_im * re], axis=1)
 
 
-def kernel(n_grp, n_fold, counts, blocks, source, res_out, image_out, alphas,
-           moves, raw, w_local, w_across, image, res, first_image, gath, edge_pack, rims, local_rhs, red,
-           load_sem, x_send, x_recv, r_send, r_recv, s_send, s_recv):
+def kernel(n_grp, n_fold, counts, blocks, source_hbm, res_out, image_out, alphas,
+           source, moves, raw, w_local, w_across, image, res, first_image, gath, edge_pack, rims, local_rhs, red,
+           source_sem, load_sem, x_send, x_recv, r_send, r_recv, s_send, s_recv):
     bf16, f32 = jnp.bfloat16, jnp.float32
     rows, comps = blocks.shape[2], blocks.shape[3]
-    nrhs = source.shape[1]
+    nrhs = source_hbm.shape[1]
     total = n_grp * n_fold
     grp, fold = lax.axis_index("grp"), lax.axis_index("fold")
     me = grp * n_fold + fold
+    fetch = pltpu.make_async_copy(source_hbm, source, source_sem)
+    fetch.start()
     loads = [pltpu.make_async_copy(blocks.at[m], raw.at[m], load_sem.at[m]) for m in range(9)]
     def device(index):
         return (lax.div(index, n_fold), lax.rem(index, n_fold))
@@ -85,6 +87,7 @@
         load.start()
 
     live = (counts[0] - 1).astype(f32)
+    fetch.wait()
 
     for p in range(2):
         planes = [source[p, k].astype(f32) for k in range(nrhs)]
@@ -395,9 +398,10 @@
     iterate = pl.pallas_call(
         functools.partial(kernel, n_grp, n_fold),
         out_shape=(held, held, jax.ShapeDtypeStruct((8, 128), f32)),
-        in_specs=[smem, pl.BlockSpec(memory_space=pl.ANY), vmem],
+        in_specs=[smem] + [pl.BlockSpec(memory_space=pltpu.HBM)] * 2,
         out_specs=(vmem, vmem, vmem),
         scratch_shapes=[
+            pltpu.VMEM(source.shape, bf16),
             pltpu.VMEM((256, 512), bf16),
             pltpu.VMEM(blocks.shape, bf16),
             pltpu.VMEM((GROUPS, rows * CHUNK, len(LOCAL) * 2 * comps), bf16),
@@ -410,6 +414,7 @@
             pltpu.VMEM((SWEEPS, 2, n_fold, 2, 6, rows, 128), bf16),
             pltpu.VMEM((5, GROUPS, 2 * comps, 256), bf16),
             pltpu.VMEM((SWEEPS, total, 1, 128), f32),
+            pltpu.SemaphoreType.DMA,
             pltpu.SemaphoreType.DMA((9,)),
             pltpu.SemaphoreType.DMA((SWEEPS, n_fold)),
             pltpu.SemaphoreType.DMA((SWEEPS, n_fold)),
@@ -420,7 +425,7 @@
         ],
         compiler_params=pltpu.CompilerParams(
             collective_id=0, has_side_effects=True, vmem_limit_bytes=52 * 1024 * 1024),
-    )(plane_counts, blocks, source)
+    )(plane_counts, blocks, pltpu.with_memory_space_constraint(source, pltpu.HBM))
     outs = pl.pallas_call(
         finish,
         out_shape=(jax.ShapeDtypeStruct(shape, f32), jax.ShapeDtypeStruct(shape, f32)),

time: 34.8 us -> 34 us (0.977)
  local copies, waits for them, and re-layouts: 0.92 us -> 0.01 us
    unnamed x2, local copies, waits for them, and re-layouts: 0.92 us -> 0.01 us
where the time goes in v5:
time: 34 us; the launch traced here: 33.8 us
  Pallas kernels  32.5 us (96%)
  between operations  1.34 us (4%)
    pallas_call x1, Pallas kernels, body(): pl.pallas_call(functools.partial(kernel, n_grp, n_fold), out_shape=(held,...  31.3 us
    pallas_call x1, Pallas kernels, body(): pl.pallas_call(finish, out_shape=(jax.ShapeDtypeStruct(shape, f32), jax.S...  1.13 us

profile of v5, /device:TPU:0, one launch (start us, length us, event | category | flops | bytes accessed | tf_op | source)
XLA Modules:
  0.0 33.8 jit_solution(3365901657423502877)
XLA Ops:
  0.6 0.0 copy-start
  1.3 31.3 %shard_map.50 = (f32[2,12,32,128]{3,2,1,0:T(8,128)S(1)}, f32[2,12,32,128]{3,2,1,0:T(8,128)S(1)}, f32[8,128]{1,0:T(8,128)S(1)}) custom-call(s32[1]{0:T(128)S(6)} %copy.5.counts, bf16[9,2,32,64,128]{4,3,2,1,0:T(8,128)(2,1)} %blocks.1, bf16[2,12,32,128]{3,2,1,0:T(8,128)(2,1)} %bitcast.3), custom_call_target="tpu_custom_call" | custom-call | tf_op jit(solution)/shard_map/pallas_call | solution.py:398
  32.7 0.0 copy-done
  32.7 1.1 %shard_map.51 = (f32[2,12,32,128]{3,2,1,0:T(8,128)}, f32[2,12,32,128]{3,2,1,0:T(8,128)}) custom-call(bf16[2,12,32,128]{3,2,1,0:T(8,128)(2,1)S(1)} %bitcast.4, f32[2,12,32,128]{3,2,1,0:T(8,128)S(1)} %get-tuple-element.7.res, f32[2,12,32,128]{3,2,1,0:T(8,128)S(1)} %get-tuple-element.8.image, f32[8,128]{1,0:T(8,128)S(1)} %get-tuple-element.9.alphas), custom_call_target="tpu_custom_call" | custom-call | tf_op jit(solution)/shard_map/pallas_call | solution.py:429
Async XLA Ops:
  0.6 32.0 %copy-start = (bf16[2,32,12,128]{3,1,2,0:T(8,128)(2,1)S(1)}, bf16[2,32,12,128]{3,1,2,0:T(8,128)(2,1)}, u32[]{:S(2)}) copy-start(bf16[2,32,12,128]{3,1,2,0:T(8,128)(2,1)} %param.4) | copy-start | bytes 589828

commit v6 on v5

--- a/solution.py
+++ b/solution.py
@@ -243,13 +243,21 @@
         return out[0] if len(out) == 1 else jnp.concatenate(out, axis=0)
 
     def apply_local(begin, end):
+        if begin < HALF < end:
+            apply_local(begin, HALF)
+            begin = HALF
+
         def chunk(g, carry):
             plane, x, low = g // HALF * HALF, g % HALF // 2, g % 2
             ahead, behind = plane + (x + 1) % 4 * 2 + low, plane + (x + 3) % 4 * 2 + low
             rhs = jnp.concatenate(
                 [local_rhs[0, g], local_rhs[0, ahead], local_rhs[0, behind]]
-                + [local_rhs[1 + hop, g] for hop in range(4)], axis=0)
-            image[g] = same_site(jnp.dot(w_local[g], rhs, preferred_element_type=f32))
+                + [local_rhs[1 + hop, g] for hop in range(4)]
+                + ([local_rhs[0, g - HALF]] if begin >= HALF else []), axis=0)
+            weights = w_local[g]
+            if begin >= HALF:
+                weights = jnp.concatenate([weights, w_across[g, :, 2 * comps:]], axis=1)
+            image[g] = same_site(jnp.dot(weights, rhs, preferred_element_type=f32))
             return carry
 
         lax.fori_loop(begin, end, chunk, 0, unroll=end - begin)
@@ -262,12 +270,11 @@
         def plane_chunk(h, after, before, sums):
             after = doubled(after[:, :128], after[:, 128:])
             before = doubled(before[:, :128], before[:, 128:])
-            inner, outer = local_rhs[0, h], local_rhs[0, h + HALF]
+            outer = local_rhs[0, h + HALF]
             up = (outer.astype(f32) * live + after.astype(f32) * (1.0 - live)).astype(bf16)
             first = same_site(jnp.dot(w_across[h], jnp.concatenate([up, before], axis=0),
                                       preferred_element_type=f32))
-            second = same_site(jnp.dot(w_across[h + HALF], jnp.concatenate([after, inner], axis=0),
-                                       preferred_element_type=f32))
+            second = same_site(jnp.dot(w_across[h + HALF, :, :2 * comps], after, preferred_element_type=f32))
             first = first + image[h]
             second = (second + image[h + HALF]) * live
             if alpha is None:
@@ -312,6 +319,10 @@
             return carry
 
         lax.fori_loop(1, total, send, 0, unroll=total <= 64)
+
+    def wait_sent(sweep):
+        everyone = red.at[sweep, pl.ds(1, total - 1)]
+        pltpu.make_async_copy(everyone, everyone, s_send.at[sweep]).wait()
 
     def wait_sums(sweep):
         everyone = red.at[sweep, pl.ds(1, total - 1)]
@@ -360,14 +371,13 @@
     send_sums(1, apply_across(first))
     natural(res, res_out)
     natural(image, image_out)
+    for copy in copies + later:
+        copy.wait_send()
+    wait_sent(0)
     second = wait_sums(1)
     alphas[...] = jnp.where(row8 == 0, first[0], jnp.where(row8 == 1, first[1], jnp.where(
         row8 == 2, second[0], jnp.where(row8 == 3, second[1], jnp.where(lane8 < 64, 1.0, live)))))
-    for copy in copies + later:
-        copy.wait_send()
-    for sweep in range(SWEEPS):
-        everyone = red.at[sweep, pl.ds(1, total - 1)]
-        pltpu.make_async_copy(everyone, everyone, s_send.at[sweep]).wait()
+    wait_sent(1)
 
 
 def finish(source, res, image, alphas, sol_out, res_out):

time: 34 us -> 33.9 us (level)
  no operation moved by 1% of the time
where the time goes in v6:
time: 33.9 us; the launch traced here: 33.8 us
  Pallas kernels  32.4 us (96%)
  between operations  1.34 us (4%)
    pallas_call x1, Pallas kernels, body(): pl.pallas_call(functools.partial(kernel, n_grp, n_fold), out_shape=(held,...  31.3 us
    pallas_call x1, Pallas kernels, body(): pl.pallas_call(finish, out_shape=(jax.ShapeDtypeStruct(shape, f32), jax.S...  1.13 us

profile of v6, /device:TPU:0, one launch (start us, length us, event | category | flops | bytes accessed | tf_op | source)
XLA Modules:
  0.0 33.8 jit_solution(12991171540361244364)
XLA Ops:
  0.6 0.0 copy-start
  1.3 31.3 %shard_map.50 = (f32[2,12,32,128]{3,2,1,0:T(8,128)S(1)}, f32[2,12,32,128]{3,2,1,0:T(8,128)S(1)}, f32[8,128]{1,0:T(8,128)S(1)}) custom-call(s32[1]{0:T(128)S(6)} %copy.5.counts, bf16[9,2,32,64,128]{4,3,2,1,0:T(8,128)(2,1)} %blocks.1, bf16[2,12,32,128]{3,2,1,0:T(8,128)(2,1)} %bitcast.3), custom_call_target="tpu_custom_call" | custom-call | tf_op jit(solution)/shard_map/pallas_call | solution.py:408
  32.6 0.0 copy-done
  32.6 1.1 %shard_map.51 = (f32[2,12,32,128]{3,2,1,0:T(8,128)}, f32[2,12,32,128]{3,2,1,0:T(8,128)}) custom-call(bf16[2,12,32,128]{3,2,1,0:T(8,128)(2,1)S(1)} %bitcast.4, f32[2,12,32,128]{3,2,1,0:T(8,128)S(1)} %get-tuple-element.7.res, f32[2,12,32,128]{3,2,1,0:T(8,128)S(1)} %get-tuple-element.8.image, f32[8,128]{1,0:T(8,128)S(1)} %get-tuple-element.9.alphas), custom_call_target="tpu_custom_call" | custom-call | tf_op jit(solution)/shard_map/pallas_call | solution.py:439
Async XLA Ops:
  0.6 32.0 %copy-start = (bf16[2,32,12,128]{3,1,2,0:T(8,128)(2,1)S(1)}, bf16[2,32,12,128]{3,1,2,0:T(8,128)(2,1)}, u32[]{:S(2)}) copy-start(bf16[2,32,12,128]{3,1,2,0:T(8,128)(2,1)} %param.4) | copy-start | bytes 589828

commit v7 on v5

--- a/solution.py
+++ b/solution.py
@@ -313,6 +313,10 @@
 
         lax.fori_loop(1, total, send, 0, unroll=total <= 64)
 
+    def wait_sent(sweep):
+        everyone = red.at[sweep, pl.ds(1, total - 1)]
+        pltpu.make_async_copy(everyone, everyone, s_send.at[sweep]).wait()
+
     def wait_sums(sweep):
         everyone = red.at[sweep, pl.ds(1, total - 1)]
         pltpu.make_async_copy(everyone, everyone, s_recv.at[sweep]).wait()
@@ -360,14 +364,13 @@
     send_sums(1, apply_across(first))
     natural(res, res_out)
     natural(image, image_out)
+    for copy in copies + later:
+        copy.wait_send()
+    wait_sent(0)
     second = wait_sums(1)
     alphas[...] = jnp.where(row8 == 0, first[0], jnp.where(row8 == 1, first[1], jnp.where(
         row8 == 2, second[0], jnp.where(row8 == 3, second[1], jnp.where(lane8 < 64, 1.0, live)))))
-    for copy in copies + later:
-        copy.wait_send()
-    for sweep in range(SWEEPS):
-        everyone = red.at[sweep, pl.ds(1, total - 1)]
-        pltpu.make_async_copy(everyone, everyone, s_send.at[sweep]).wait()
+    wait_sent(1)
 
 
 def finish(source, res, image, alphas, sol_out, res_out):

time: 34 us -> 33.9 us (level)
  no operation moved by 1% of the time
where the time goes in v7:
time: 33.9 us; the launch traced here: 33.8 us
  Pallas kernels  32.4 us (96%)
  between operations  1.34 us (4%)
    pallas_call x1, Pallas kernels, body(): pl.pallas_call(functools.partial(kernel, n_grp, n_fold), out_shape=(held,...  31.3 us
    pallas_call x1, Pallas kernels, body(): pl.pallas_call(finish, out_shape=(jax.ShapeDtypeStruct(shape, f32), jax.S...  1.13 us

profile of v7, /device:TPU:0, one launch (start us, length us, event | category | flops | bytes accessed | tf_op | source)
XLA Modules:
  0.0 33.8 jit_solution(17488144673117336554)
XLA Ops:
  0.6 0.0 copy-start
  1.3 31.3 %shard_map.50 = (f32[2,12,32,128]{3,2,1,0:T(8,128)S(1)}, f32[2,12,32,128]{3,2,1,0:T(8,128)S(1)}, f32[8,128]{1,0:T(8,128)S(1)}) custom-call(s32[1]{0:T(128)S(6)} %copy.5.counts, bf16[9,2,32,64,128]{4,3,2,1,0:T(8,128)(2,1)} %blocks.1, bf16[2,12,32,128]{3,2,1,0:T(8,128)(2,1)} %bitcast.3), custom_call_target="tpu_custom_call" | custom-call | tf_op jit(solution)/shard_map/pallas_call | solution.py:401
  32.6 0.0 copy-done
  32.7 1.1 %shard_map.51 = (f32[2,12,32,128]{3,2,1,0:T(8,128)}, f32[2,12,32,128]{3,2,1,0:T(8,128)}) custom-call(bf16[2,12,32,128]{3,2,1,0:T(8,128)(2,1)S(1)} %bitcast.4, f32[2,12,32,128]{3,2,1,0:T(8,128)S(1)} %get-tuple-element.7.res, f32[2,12,32,128]{3,2,1,0:T(8,128)S(1)} %get-tuple-element.8.image, f32[8,128]{1,0:T(8,128)S(1)} %get-tuple-element.9.alphas), custom_call_target="tpu_custom_call" | custom-call | tf_op jit(solution)/shard_map/pallas_call | solution.py:432
Async XLA Ops:
  0.6 32.0 %copy-start = (bf16[2,32,12,128]{3,1,2,0:T(8,128)(2,1)S(1)}, bf16[2,32,12,128]{3,1,2,0:T(8,128)(2,1)}, u32[]{:S(2)}) copy-start(bf16[2,32,12,128]{3,1,2,0:T(8,128)(2,1)} %param.4) | copy-start | bytes 589828
